TPU v7x, 32 devices: a whole 2x2x4 slice. The times are simulated.
32 devices in a mesh: ctx: 4 (over y, core), tp: 8 (over z, x).
Axes of the slice: x: 2, y: 2, z: 4, core: 2. Of those that a mesh axis runs over, the one named last changes fastest.
Arguments:
- query_in: bfloat16 [4096, 8192], P('ctx', 'tp'), may hold values from -6 to 6
- key_in: bfloat16 [4096, 8192], P('ctx', 'tp'), may hold values from -6 to 6
- value_in: bfloat16 [4096, 8192], P('ctx', 'tp'), may hold values from -6 to 6
- short_taps: float32 [3, 7, 8192], P(None, None, 'tp'), may hold values from -2 to 2
- modal_poles: float32 [16, 8192], P(None, 'tp'), may hold values from 0 to 1, as said below
- modal_residues: float32 [16, 8192], P(None, 'tp'), may hold values from -0.5 to 0.5
- out_weight: bfloat16 [8192, 8192], P('tp'), may hold values from -0.0625 to 0.0625
- grad_out: bfloat16 [4096, 8192], P('ctx', 'tp'), may hold values from -6 to 6
Outputs:
- gated: bfloat16 [4096, 8192], P('ctx', 'tp')
- grad_query: bfloat16 [4096, 8192], P('ctx', 'tp')
- grad_key: bfloat16 [4096, 8192], P('ctx', 'tp')
- grad_value: bfloat16 [4096, 8192], P('ctx', 'tp')
Inputs may be any that keep to these rules, and one draw needn't show every extreme that they name: `modal_poles`: every pole lies strictly between 0 and 1.
All inputs are finite; a program needn't handle non-finite values.
Results may differ from a plain program's by a relative error of at most 0.0017.
Values may be sent and summed in bfloat16 or wider, within the bound.
A program may use at most 192 MiB of HBM per device.

v0:
```python
import jax
import jax.numpy as jnp
from jax import lax
from jax.sharding import PartitionSpec as P

HIGHEST = lax.Precision.HIGHEST


def entering_2(value, axis, join, neutral, backward):
    count, mine = (lax.axis_size(axis), lax.axis_index(axis))
    pieces = jax.tree.map(lambda part: lax.all_gather(part, axis), value)
    if backward:
        pieces = jax.tree.map(lambda part: part[::-1], pieces)
        mine = count - 1 - mine
    subtotal = jax.tree.map(
        lambda part, zero: jnp.full_like(part, 0) + jnp.asarray(zero, part.dtype), value, neutral
    )

    def lap(position, subtotal):
        longer = join(subtotal, jax.tree.map(lambda part: part[position], pieces))
        return jax.tree.map(lambda new, old: jnp.where(position < mine, new, old), longer, subtotal)

    return lax.fori_loop(0, count - 1, lap, subtotal)


def from_behind(block, axis, distance):
    devices = range(lax.axis_size(axis))
    route = [(i - distance, i) for i in devices if i - distance in devices]
    return lax.ppermute(block, axis, route)


def toeplitz_rows(kernel):
    block = kernel.shape[0]
    chan_width = kernel.shape[1]
    flipped = jnp.concatenate(
        [kernel.T[:, ::-1], jnp.zeros((chan_width, block - 1), kernel.dtype)], axis=1
    )
    repeated = jnp.tile(flipped, (1, block + 1))[:, : block * 2 * block]
    hankel = repeated.reshape(chan_width, block, 2 * block)[:, :, :block]
    return hankel[:, ::-1, :]


def link_states(earlier, later):
    return (earlier[0] * later[0], later[0] * earlier[1] + later[1])


def carry_states(own_state, log_poles, tok_rows, backward):
    full_decay = jnp.exp(tok_rows * log_poles)
    unit_item = (jnp.ones_like(own_state), jnp.zeros_like(own_state))
    result = entering_2((full_decay, own_state), "ctx", link_states, unit_item, backward)
    return result[1]


def shards(
    query_in, key_in, value_in, short_taps, modal_poles, modal_residues, out_weight, grad_out
):
    tap_count = short_taps.shape[1]
    rim_rows = tap_count - 1
    tok_rows = query_in.shape[0]
    chan_width = query_in.shape[1]
    stacked = jnp.stack([query_in, key_in, value_in])
    prior = from_behind(stacked[:, tok_rows - rim_rows :, :], "ctx", 1)
    extended = jnp.concatenate([prior, stacked], axis=1).astype(jnp.float32)
    filtered = jnp.zeros((3, tok_rows, chan_width), jnp.float32)
    for tap_index in range(tap_count):
        begin = rim_rows - tap_index
        filtered = (
            filtered + short_taps[:, tap_index, None, :] * extended[:, begin : begin + tok_rows, :]
        )
    q_short = filtered[0]
    k_short = filtered[1]
    v_short = filtered[2]
    product = k_short * v_short
    log_poles = jnp.log(modal_poles)
    block = min(64, tok_rows)
    block_count = tok_rows // block
    lag_steps = jnp.arange(block, dtype=jnp.float32)
    powers = jnp.exp(lag_steps[:, None, None] * log_poles[None])
    kernel = jnp.einsum("dmc,mc->dc", powers, modal_residues, precision=HIGHEST)
    toeplitz_mat = toeplitz_rows(kernel)
    block_index = jnp.arange(block_count, dtype=jnp.float32)
    block_gap = block_index[:, None] - block_index[None, :] - 1.0
    gap_decay = jnp.exp(
        jnp.maximum(block_gap, 0.0)[:, :, None, None] * block * log_poles[None, None]
    )
    decay_mat = jnp.where(block_gap[:, :, None, None] >= 0.0, gap_decay, 0.0)
    from_start = jnp.exp(block_index[:, None, None] * block * log_poles[None])
    to_finish = jnp.exp((block_count - 1.0 - block_index)[:, None, None] * block * log_poles[None])
    u_blocks = product.reshape(block_count, block, chan_width)
    local_part = jnp.einsum("cij,njc->nic", toeplitz_mat, u_blocks, precision=HIGHEST)
    block_ends = jnp.einsum("jmc,njc->nmc", powers[::-1], u_blocks, precision=HIGHEST)
    own_end = jnp.sum(to_finish * block_ends, axis=0)
    state_before = carry_states(own_end, log_poles, tok_rows, False)
    entering = (
        jnp.einsum("nkmc,kmc->nmc", decay_mat, block_ends, precision=HIGHEST)
        + from_start * state_before[None]
    )
    lead_terms = jnp.exp((lag_steps + 1.0)[:, None, None] * log_poles[None]) * modal_residues[None]
    long_out = (
        local_part + jnp.einsum("imc,nmc->nic", lead_terms, entering, precision=HIGHEST)
    ).reshape(tok_rows, chan_width)
    gated = (q_short * long_out).astype(jnp.bfloat16)
    grad_mixed = lax.dot_general(
        lax.all_gather(grad_out, "tp", axis=1, tiled=True),
        out_weight,
        (((1,), (1,)), ((), ())),
        preferred_element_type=jnp.float32,
    )
    grad_qs = grad_mixed * long_out
    grad_long = grad_mixed * q_short
    grad_blocks = grad_long.reshape(block_count, block, chan_width)
    back_local = jnp.einsum("cij,nic->njc", toeplitz_mat, grad_blocks, precision=HIGHEST)
    block_starts = jnp.einsum("imc,nic->nmc", powers, grad_blocks, precision=HIGHEST)
    own_start = jnp.sum(from_start * block_starts, axis=0)
    state_after = carry_states(own_start, log_poles, tok_rows, True)
    leaving = (
        jnp.einsum("knmc,kmc->nmc", decay_mat, block_starts, precision=HIGHEST)
        + to_finish * state_after[None]
    )
    trail_terms = (
        jnp.exp((block - lag_steps)[:, None, None] * log_poles[None]) * modal_residues[None]
    )
    grad_product = (
        back_local + jnp.einsum("jmc,nmc->njc", trail_terms, leaving, precision=HIGHEST)
    ).reshape(tok_rows, chan_width)
    grad_ks = grad_product * v_short
    grad_vs = grad_product * k_short
    grads = jnp.stack([grad_qs, grad_ks, grad_vs])
    later = from_behind(grads[:, :rim_rows, :], "ctx", -1)
    grads_ext = jnp.concatenate([grads, later], axis=1)
    returned = jnp.zeros((3, tok_rows, chan_width), jnp.float32)
    for tap_index in range(tap_count):
        returned = (
            returned
            + short_taps[:, tap_index, None, :] * grads_ext[:, tap_index : tap_index + tok_rows, :]
        )
    return (
        gated,
        returned[0].astype(jnp.bfloat16),
        returned[1].astype(jnp.bfloat16),
        returned[2].astype(jnp.bfloat16),
    )


def solution(mesh):
    placed = (
        P("ctx", "tp"),
        P("ctx", "tp"),
        P("ctx", "tp"),
        P(None, None, "tp"),
        P(None, "tp"),
        P(None, "tp"),
        P("tp", None),
        P("ctx", "tp"),
    )
    return jax.shard_map(
        shards,
        mesh=mesh,
        in_specs=placed,
        out_specs=(P("ctx", "tp"), P("ctx", "tp"), P("ctx", "tp"), P("ctx", "tp")),
        check_vma=False,
    )
```

profile of v0, /device:TPU:1, one launch (start us, length us, event | category | flops | bytes accessed | tf_op | source)
XLA Modules:
  0.0 572.7 jit_solution(1259244511439853776)
XLA Ops:
  7.2 0.7 all-gather.5.cloned.1.call-update
  7.9 0.8 pad_maximum_fusion.2
  8.7 4.5 collective-permute-start
  13.3 0.2 copy.64
  13.5 0.2 copy.108
  13.7 0.6 iota_add_fusion
  14.3 0.6 iota_subtract_fusion
  14.9 0.5 subtract_multiply_fusion
  15.7 6.1 %multiply_exponential_fusion.4 = f32[64,16,1024]{0,1,2:T(8,128)} fusion(f32[16,1024]{0,1:T(8,128)S(1)} %copy.64), kind=kLoop, calls=%fused_computation.58 | loop fusion | flops 1048576 | bytes 4259840 | tf_op jit(solution)/shard_map/exp | solution.py:78
  21.8 11.7 %multiply_reduce_fusion.2 = f32[1024,64]{1,0:T(8,128)S(1)} fusion(f32[1024,16]{1,0:T(8,128)S(1)} %copy.108, f32[16,1024]{0,1:T(8,128)S(1)} %copy.64), kind=kLoop, calls=%fused_computation.45 | loop fusion | flops 3080192 | bytes 393216
  33.5 5.0 all-gather
  38.6 1.0 copy.71
  39.6 0.7 rev.18
  40.3 0.2 copy.83
  40.5 0.2 rev.15
  40.7 13.1 %rev.17 = f32[64,16,1024]{0,1,2:T(8,128)} reverse(f32[64,16,1024]{0,1,2:T(8,128)} %multiply_exponential_fusion.4), dimensions={0} | reverse | bytes 8388608 | tf_op jit(solution)/shard_map/rev | solution.py:91
  53.9 11.5 %tile.4 = f32[1024,65,127]{0,2,1:T(8,128)} broadcast(f32[1024,127]{0,1:T(8,128)S(1)} %concatenate.10), dimensions={0,2} | broadcast | bytes 34332672 | tf_op jit(solution)/shard_map/tile | solution.py:38
  65.4 23.7 %tile.10 = f32[1024,8255]{0,1:T(8,128)} reshape(f32[1024,65,127]{0,2,1:T(8,128)} %tile.4) | data formatting | bytes 67624960 | tf_op jit(solution)/shard_map/tile | solution.py:38
  89.0 10.6 %slice-done = f32[1024,8192]{0,1:T(8,128)S(1)} async-done(((f32[1024,8255]{0,1:T(8,128)}), f32[1024,8192]{0,1:T(8,128)S(1)}, s32[]{:S(2)}) %slice-start) | async-done | bytes 33554456 | tf_op jit(solution)/shard_map/slice | solution.py:38
  99.6 6.9 %slice.141 = f32[1024,64,64]{0,2,1:T(8,128)} slice(f32[1024,64,128]{0,2,1:T(8,128)S(1)} %bitcast.110), slice={[0:1024], [0:64], [0:64]} | slice | bytes 33554432 | tf_op jit(solution)/shard_map/slice | solution.py:39
  106.5 30.5 %copy.107 = f32[1024,64,64]{2,1,0:T(8,128)} copy(f32[1024,64,64]{0,2,1:T(8,128)} %slice.141) | data formatting | bytes 33554432
  137.0 43.2 %rev.16 = f32[1024,64,64]{2,1,0:T(8,128)} reverse(f32[1024,64,64]{2,1,0:T(8,128)} %copy.107), dimensions={1} | reverse | bytes 33554432 | tf_op jit(solution)/shard_map/rev | solution.py:40
  180.3 7.1 %maximum_convert_fusion = f32[3,1030,1024]{2,1,0:T(8,128)} fusion(bf16[1,1024,1024]{2,1,0:T(8,128)(2,1)S(1)} %bitcast.121, bf16[1,1024,1024]{2,1,0:T(8,128)(2,1)} %bitcast.123, bf16[1,1024,1024]{2,1,0:T(8,128)(2,1)} %bitcast.125, bf16[3,6,1024]{2,1,0:T(8,128)(2,1)S(1)} %collective-permute-done), kind=kLoop, calls=%fused_computation.60 | loop fusion | flops 25313280 | bytes 18984960 | tf_op jit(solution)/shard_map/convert_element_type | solution.py:63
  187.4 35.5 %fusion.9 = f32[3,1024,1024]{2,1,0:T(8,128)} fusion(f32[3,1030,1024]{2,1,0:T(8,128)} %maximum_convert_fusion, f32[3,1024]{1,0:T(4,128)S(1)} %get-tuple-element.276, f32[3,1024]{1,0:T(4,128)S(1)} %get-tuple-element.277, f32[3,1024]{1,0:T(4,128)S(1)} %get-tuple-element.278, f32[3,1024]{1,0:T(4,128)S(1)} %get-tuple-element.279, ...), kind=kLoop, calls=%fused_computation.24 | loop fusion | flops 40894464 | bytes 100749312 | tf_op jit(solution)/shard_map/add | solution.py:68
  222.9 6.9 %slice_multiply_fusion.13 = f32[1,1024,1024]{2,1,0:T(8,128)} fusion(f32[3,1024,1024]{2,1,0:T(8,128)} %fusion.9), kind=kLoop, calls=%fused_computation.81 | loop fusion | flops 1048576 | bytes 12582912 | tf_op jit(solution)/shard_map/mul | solution.py:73
  229.8 8.1 %copy.66 = f32[16,64,1024]{1,0,2:T(8,128)} copy(f32[16,64,1024]{2,1,0:T(8,128)} %bitcast.119) | data formatting | bytes 8388608 | tf_op jit(solution)/shard_map/mul | solution.py:73
  237.9 19.3 %fusion.45 = f32[1024,16,16]{2,1,0:T(8,128)} fusion(f32[16,64,1024]{1,0,2:T(8,128)} %copy.66, f32[64,16,1024]{0,1,2:T(8,128)} %rev.17), kind=kOutput, calls=%fused_computation.103 | convolution fusion | flops 201326592 | bytes 9437184 | tf_op jit(solution)/shard_map/jmc,njc->nmc/dot_general | solution.py:91
  257.2 5.1 copy.109
  262.3 4.9 multiply_reduce_fusion.1
  267.1 6.2 %copy.91 = f32[16,1024,16]{0,2,1:T(8,128)} copy(f32[16,1024,16]{1,0,2:T(8,128)S(1)} %multiply_reduce_fusion.1) | data formatting | bytes 2097152 | tf_op jit(solution)/shard_map/nkmc,kmc->nmc/dot_general | solution.py:95
  273.3 27.4 %fusion.42 = (f32[1024,1024]{1,0:T(8,128)}, f32[1024,1024]{1,0:T(8,128)}) fusion(f32[3,1024,1024]{2,1,0:T(8,128)} %fusion.9, bf16[1024,8192]{1,0:T(8,128)(2,1)} %all-gather.5.cloned.1.call-done, bf16[1024,8192]{1,0:T(8,128)(2,1)} %param.18), kind=kOutput, calls=%fused_computation.80 | convolution fusion | flops 17180917760 | bytes 46137344 | tf_op jit(solution)/shard_map/dot_general | solution.py:103
  300.8 8.2 %copy.73 = f32[16,64,1024]{1,0,2:T(8,128)} copy(f32[16,64,1024]{2,1,0:T(8,128)} %bitcast.126) | data formatting | bytes 8388608 | tf_op jit(solution)/shard_map/reshape | solution.py:111
  309.0 21.5 %fusion.16 = (f32[16,1024]{0,1:T(8,128)S(1)}, f32[16,1024]{0,1:T(8,128)S(1)}, f32[1024,16,16]{2,1,0:T(8,128)}) fusion(f32[16,1024]{0,1:T(8,128)S(1)} %copy-done.5, f32[16]{0:T(128)S(1)} %copy-done.29, f32[1024,16,16]{2,1,0:T(8,128)} %fusion.45, f32[16]{0:T(128)S(1)} %copy-done.30, f32[16,64,1024]{1,0,2:T(8,128)} %copy.73), kind=kOutput, calls=%fused_computation.40 | convolution fusion | flops 203915264 | bytes 6488192 | tf_op jit(solution)/shard_map/imc,nic->nmc/dot_general | solution.py:113
  330.5 0.2 copy.75
  330.7 0.2 copy.69
  330.8 6.0 %all-gather.1 = f32[64,1024]{1,0:T(8,128)S(1)} all-gather(f32[16,1024]{1,0:T(8,128)S(1)} %copy.69), channel_id=3, replica_groups=mesh['ctx'=4,'tp'=8] {'ctx'}, dimensions={0}, use_global_device_ids=true | all-gather | bytes 327680 | tf_op jit(solution)/shard_map/all_gather | solution.py:11
  336.8 2.7 while.28
  336.8 0.9 fusion.57
  337.7 0.9 fusion.57
  338.6 0.9 fusion.57
  339.5 5.9 %all-gather.2 = f32[64,1024]{1,0:T(8,128)S(1)} all-gather(f32[16,1024]{1,0:T(8,128)S(1)} %copy.75), channel_id=4, replica_groups=mesh['ctx'=4,'tp'=8] {'ctx'}, dimensions={0}, use_global_device_ids=true | all-gather | bytes 327680 | tf_op jit(solution)/shard_map/all_gather | solution.py:11
  345.4 2.9 while.29
  345.6 0.9 fusion.58
  346.5 0.9 fusion.58
  347.4 0.9 fusion.58
  348.3 1.0 copy.76
  349.3 1.0 copy.70
  350.3 5.1 copy.110
  355.4 4.2 multiply_reduce_fusion
  359.6 6.2 %copy.99 = f32[16,1024,16]{0,2,1:T(8,128)} copy(f32[16,1024,16]{1,0,2:T(8,128)S(1)} %multiply_reduce_fusion) | data formatting | bytes 2097152 | tf_op jit(solution)/shard_map/knmc,kmc->nmc/dot_general | solution.py:117
  365.9 15.3 %fusion.15 = f32[1024,16,64]{2,1,0:T(8,128)S(1)} fusion(f32[16,1024,16]{0,2,1:T(8,128)} %copy.99, f32[64]{0:T(128)S(1)} %copy-done.32, f32[16,1024]{0,1:T(8,128)S(1)} %copy-done.11, f32[16,1024]{0,1:T(8,128)S(1)} %copy-done.9, f32[16]{0:T(128)S(1)} %copy-done.30, f32[16,1024]{0,1:T(8,128)S(1)} %copy-done.5), kind=kOutput, calls=%fused_computation.38 | convolution fusion | flops 204210176 | bytes 5439808 | tf_op jit(solution)/shard_map/jmc,nmc->njc/dot_general | solution.py:124
  381.2 33.9 %add_bitcast_fusion = f32[16,64,1024]{1,0,2:T(8,128)} fusion(f32[1024,16,64]{2,1,0:T(8,128)S(1)} %fusion.15, f32[16,64,1024]{1,0,2:T(8,128)} %copy.73, f32[1024,64,64]{2,1,0:T(8,128)} %rev.16), kind=kOutput, calls=%fused_computation.46 | convolution fusion | flops 806354944 | bytes 29360128 | tf_op jit(solution)/shard_map/cij,nic->njc/dot_general | solution.py:112
  415.1 15.2 %fusion.17 = f32[1024,16,64]{2,1,0:T(8,128)S(1)} fusion(f32[16,1024,16]{0,2,1:T(8,128)} %copy.91, f32[16,1024]{0,1:T(8,128)S(1)} %copy-done.9, f32[64]{0:T(128)S(1)} %copy-done.31, f32[16,1024]{0,1:T(8,128)S(1)} %copy-done.10, f32[16,1024]{0,1:T(8,128)S(1)} %copy-done.5, f32[16]{0:T(128)S(1)} %copy-done.29), kind=kOutput, calls=%fused_computation.42 | convolution fusion | flops 204210176 | bytes 5439808 | tf_op jit(solution)/shard_map/imc,nmc->nic/dot_general | solution.py:100
  430.3 57.3 %add_bitcast_fusion.1 = f32[16,64,1024]{1,0,2:T(8,128)} fusion(f32[1024,16,64]{2,1,0:T(8,128)S(1)} %fusion.17, f32[16,64,1024]{1,0,2:T(8,128)S(1)} %bitcast.112, f32[1024,64,64]{2,1,0:T(8,128)} %rev.16), kind=kOutput, calls=%fused_computation.51 | convolution fusion | flops 806354944 | bytes 29360128 | tf_op jit(solution)/shard_map/cij,njc->nic/dot_general | solution.py:90
  487.6 6.9 %copy.72 = f32[16,64,1024]{2,1,0:T(8,128)} copy(f32[16,64,1024]{1,0,2:T(8,128)} %add_bitcast_fusion.1) | data formatting | bytes 8388608 | tf_op jit(solution)/shard_map/add | solution.py:100
  494.4 7.0 %copy.77 = f32[16,64,1024]{2,1,0:T(8,128)} copy(f32[16,64,1024]{1,0,2:T(8,128)} %add_bitcast_fusion) | data formatting | bytes 8388608 | tf_op jit(solution)/shard_map/add | solution.py:124
  501.5 6.4 %bitcast_multiply_fusion.5 = (f32[1,1024,1024]{2,1,0:T(8,128)S(1)}, f32[1,1024,1024]{2,1,0:T(8,128)S(1)}) fusion(f32[3,1024,1024]{2,1,0:T(8,128)} %fusion.9, f32[1,1024,1024]{2,1,0:T(8,128)} %bitcast.118), kind=kLoop, calls=%fused_computation.63 | loop fusion | flops 2097152 | bytes 20971520 | tf_op jit(solution)/shard_map/mul | solution.py:126
  507.9 7.5 %bitcast_multiply_fusion.6 = (f32[1024,1024]{1,0:T(8,128)S(1)}, bf16[1024,1024]{1,0:T(8,128)(2,1)}) fusion(f32[1024,1024]{1,0:T(8,128)} %get-tuple-element.274, f32[16,64,1024]{2,1,0:T(8,128)S(1)} %copy-done.2, f32[3,1024,1024]{2,1,0:T(8,128)} %fusion.9), kind=kLoop, calls=%fused_computation.64 | loop fusion | flops 3145728 | bytes 18874368 | tf_op jit(solution)/shard_map/mul | solution.py:109
  515.4 1.3 pad_maximum_fusion.1
  516.7 2.2 collective-permute-start.1
  519.0 3.9 collective-permute-done.1
  522.8 5.5 pad_maximum_fusion
  528.4 31.3 %fusion.3 = bf16[3,1024,1024]{2,1,0:T(8,128)(2,1)} fusion(f32[3,1030,1024]{2,1,0:T(8,128)} %pad_maximum_fusion, f32[3,1024]{1,0:T(4,128)S(1)} %copy-done.22, f32[3,1024]{1,0:T(4,128)S(1)} %copy-done.24, f32[3,1024]{1,0:T(4,128)S(1)} %copy-done.14, f32[3,1024]{1,0:T(4,128)S(1)} %copy-done.16, f32[3,1024]{1,0:T(4,128)S(1)} %copy-done.18, ...), kind=kLoop, calls=%fused_computation.12 | loop fusion | flops 50331648 | bytes 94457856 | tf_op jit(solution)/shard_map/convert.2
  559.7 5.7 %slice_bitcast_fusion.1 = (bf16[1024,1024]{1,0:T(8,128)(2,1)}, bf16[1024,1024]{1,0:T(8,128)(2,1)}, bf16[1024,1024]{1,0:T(8,128)(2,1)}) fusion(bf16[3,1024,1024]{2,1,0:T(8,128)(2,1)} %fusion.3), kind=kLoop, calls=%fused_computation.82 | loop fusion | bytes 12582912 | tf_op jit(solution)/shard_map/convert_element_type | solution.py:141
  (88 shorter events, 0.4 us)
Async XLA Ops:
  7.2 6.1 %copy-start.28 = (f32[16,1024]{1,0:T(8,128)S(1)}, f32[16,1024]{1,0:T(8,128)}, u32[]{:S(2)}) copy-start(f32[16,1024]{1,0:T(8,128)} %param.16) | copy-start | bytes 196612
  7.2 6.3 %copy-start.12 = (f32[16,1024]{1,0:T(8,128)S(1)}, f32[16,1024]{1,0:T(8,128)}, u32[]{:S(2)}) copy-start(f32[16,1024]{1,0:T(8,128)} %param.17) | copy-start | bytes 196612
  7.2 8.3 %copy-start.27 = (f32[3,7,1024]{2,1,0:T(8,128)S(1)}, f32[3,7,1024]{2,1,0:T(8,128)}, u32[]{:S(2)}) copy-start(f32[3,7,1024]{2,1,0:T(8,128)} %param.15) | copy-start | bytes 258052
  7.2 266.1 %all-gather.5.cloned.1.call-start = ((), (), s32[]{:S(2)}) async-start(), calls=%async_computation | async-start | bytes 18874368 | tf_op jit(solution)/shard_map/all_gather | solution.py:104
  8.7 171.5 %collective-permute-start = (bf16[3,6,1024]{2,1,0:T(8,128)(2,1)S(1)}, bf16[3,6,1024]{2,1,0:T(8,128)(2,1)S(1)}, u32[]{:S(2)}, u32[]{:S(2)}) collective-permute-start(bf16[3,6,1024]{2,1,0:T(8,128)(2,1)S(1)} %pad_maximum_fusion.2), channel_id=1, source_target_pairs={{0,8},{8,16},{16,24},{1,9},{9,17},{17,25},{2,10},{10,18},{18,26},{... | collective-permute-start | bytes 110600 | tf_op jit(solution)/shard_map/ppermute | solution.py:29
  13.5 40.3 %copy-start.4 = (f32[16,1024]{0,1:T(8,128)}, f32[16,1024]{0,1:T(8,128)S(1)}, u32[]{:S(2)}) copy-start(f32[16,1024]{0,1:T(8,128)S(1)} %copy.64) | copy-start | bytes 196612
  15.6 171.8 %copy-start.13 = (f32[3,1024]{1,0:T(4,128)}, f32[3,1024]{1,0:T(4,128)S(1)}, u32[]{:S(2)}) copy-start(f32[3,1024]{1,0:T(4,128)S(1)} %get-tuple-element.278) | copy-start | bytes 36868
  15.6 171.8 %copy-start.15 = (f32[3,1024]{1,0:T(4,128)}, f32[3,1024]{1,0:T(4,128)S(1)}, u32[]{:S(2)}) copy-start(f32[3,1024]{1,0:T(4,128)S(1)} %get-tuple-element.279) | copy-start | bytes 36868
  15.6 171.8 %copy-start.17 = (f32[3,1024]{1,0:T(4,128)}, f32[3,1024]{1,0:T(4,128)S(1)}, u32[]{:S(2)}) copy-start(f32[3,1024]{1,0:T(4,128)S(1)} %get-tuple-element.280) | copy-start | bytes 36868
  15.6 171.8 %copy-start.19 = (f32[3,1024]{1,0:T(4,128)}, f32[3,1024]{1,0:T(4,128)S(1)}, u32[]{:S(2)}) copy-start(f32[3,1024]{1,0:T(4,128)S(1)} %get-tuple-element.281) | copy-start | bytes 36868
  15.6 171.7 %copy-start.21 = (f32[3,1024]{1,0:T(4,128)}, f32[3,1024]{1,0:T(4,128)S(1)}, u32[]{:S(2)}) copy-start(f32[3,1024]{1,0:T(4,128)S(1)} %get-tuple-element.276) | copy-start | bytes 36868
  15.7 171.7 %copy-start.23 = (f32[3,1024]{1,0:T(4,128)}, f32[3,1024]{1,0:T(4,128)S(1)}, u32[]{:S(2)}) copy-start(f32[3,1024]{1,0:T(4,128)S(1)} %get-tuple-element.277) | copy-start | bytes 36868
  38.6 15.3 %copy-start.6 = (f32[64,1024]{1,0:T(8,128)}, f32[64,1024]{1,0:T(8,128)S(1)}, u32[]{:S(2)}) copy-start(f32[64,1024]{1,0:T(8,128)S(1)} %all-gather) | copy-start | bytes 786436
  39.6 147.8 %copy-start.25 = (f32[3,1,1024]{2,0,1:T(4,128)}, f32[3,1,1024]{2,0,1:T(4,128)S(1)}, u32[]{:S(2)}) copy-start(f32[3,1,1024]{2,0,1:T(4,128)S(1)} %copy.120) | copy-start | bytes 36868
  89.0 10.6 %slice-start = ((f32[1024,8255]{0,1:T(8,128)}), f32[1024,8192]{0,1:T(8,128)S(1)}, s32[]{:S(2)}) async-start(f32[1024,8255]{0,1:T(8,128)} %tile.10), calls=%async_computation.1 | async-start | bytes 67108864 | tf_op jit(solution)/shard_map/slice | solution.py:38
  137.0 43.3 %copy-start.3 = (bf16[1024,1024]{1,0:T(8,128)(2,1)S(1)}, bf16[1024,1024]{1,0:T(8,128)(2,1)}, u32[]{:S(2)}) copy-start(bf16[1024,1024]{1,0:T(8,128)(2,1)} %param.14) | copy-start | bytes 6291460
  300.8 8.2 %copy-start.5 = (f32[16,1024]{0,1:T(8,128)S(1)}, f32[16,1024]{0,1:T(8,128)}, u32[]{:S(2)}) copy-start(f32[16,1024]{0,1:T(8,128)} %copy-done.4) | copy-start | bytes 196612
  300.8 8.2 %copy-start.29 = (f32[16]{0:T(128)S(1)}, f32[16]{0:T(128)}, u32[]{:S(2)}) copy-start(f32[16]{0:T(128)} %get-tuple-element.283) | copy-start | bytes 196
  300.8 8.2 %copy-start.30 = (f32[16]{0:T(128)S(1)}, f32[16]{0:T(128)}, u32[]{:S(2)}) copy-start(f32[16]{0:T(128)} %get-tuple-element.282) | copy-start | bytes 196
  309.0 27.9 %copy-start.8 = (f32[16,1024]{1,0:T(8,128)S(1)}, f32[16,1024]{1,0:T(8,128)}, u32[]{:S(2)}) copy-start(f32[16,1024]{1,0:T(8,128)} %custom-call) | copy-start | bytes 196612
  309.0 36.4 %copy-start.7 = (f32[16,1024]{1,0:T(8,128)S(1)}, f32[16,1024]{1,0:T(8,128)}, u32[]{:S(2)}) copy-start(f32[16,1024]{1,0:T(8,128)} %custom-call.1) | copy-start | bytes 196612
  355.4 10.4 %copy-start.9 = (f32[16,1024]{0,1:T(8,128)S(1)}, f32[16,1024]{0,1:T(8,128)}, u32[]{:S(2)}) copy-start(f32[16,1024]{0,1:T(8,128)} %copy.71) | copy-start | bytes 196612
  355.4 10.4 %copy-start.32 = (f32[64]{0:T(128)S(1)}, f32[64]{0:T(128)}, u32[]{:S(2)}) copy-start(f32[64]{0:T(128)} %iota_subtract_fusion) | copy-start | bytes 772
  359.6 6.2 %copy-start.11 = (f32[16,1024]{0,1:T(8,128)S(1)}, f32[16,1024]{0,1:T(8,128)}, u32[]{:S(2)}) copy-start(f32[16,1024]{0,1:T(8,128)} %copy.76) | copy-start | bytes 196612
  365.8 64.4 %slice-start.1 = ((s8[8388608]{0:T(1024)(128)(4,1)}), s8[4194304]{0:T(1024)(128)(4,1)S(1)}, s32[]{:S(2)}) async-start(s8[8388608]{0:T(1024)(128)(4,1)} %bitcast.111), calls=%async_computation.2 | async-start | bytes 8388608
  381.2 33.9 %copy-start.10 = (f32[16,1024]{0,1:T(8,128)S(1)}, f32[16,1024]{0,1:T(8,128)}, u32[]{:S(2)}) copy-start(f32[16,1024]{0,1:T(8,128)} %copy.70) | copy-start | bytes 196612
  381.2 33.9 %copy-start.31 = (f32[64]{0:T(128)S(1)}, f32[64]{0:T(128)}, u32[]{:S(2)}) copy-start(f32[64]{0:T(128)} %iota_add_fusion) | copy-start | bytes 772
  381.2 49.1 %slice-start.2 = ((s8[8388608]{0:T(1024)(128)(4,1)}), s8[4194304]{0:T(1024)(128)(4,1)S(1)}, s32[]{:S(2)}) async-start(s8[8388608]{0:T(1024)(128)(4,1)} %bitcast.111), calls=%async_computation.3 | async-start | bytes 8388608
  501.5 6.4 %copy-start.2 = (f32[16,64,1024]{2,1,0:T(8,128)S(1)}, f32[16,64,1024]{2,1,0:T(8,128)}, u32[]{:S(2)}) copy-start(f32[16,64,1024]{2,1,0:T(8,128)} %copy.72) | copy-start | bytes 12582916
  507.9 15.0 %copy-start = (f32[1,1024,1024]{2,1,0:T(8,128)}, f32[1,1024,1024]{2,1,0:T(8,128)S(1)}, u32[]{:S(2)}) copy-start(f32[1,1024,1024]{2,1,0:T(8,128)S(1)} %get-tuple-element.258) | copy-start | bytes 12582916
  515.4 7.4 %copy-start.1 = (f32[1024,1024]{1,0:T(8,128)}, f32[1024,1024]{1,0:T(8,128)S(1)}, u32[]{:S(2)}) copy-start(f32[1024,1024]{1,0:T(8,128)S(1)} %get-tuple-element.262) | copy-start | bytes 12582916
  516.7 11.7 %copy-start.14 = (f32[3,1024]{1,0:T(4,128)S(1)}, f32[3,1024]{1,0:T(4,128)}, u32[]{:S(2)}) copy-start(f32[3,1024]{1,0:T(4,128)} %copy-done.13) | copy-start | bytes 36868
  516.7 11.7 %copy-start.16 = (f32[3,1024]{1,0:T(4,128)S(1)}, f32[3,1024]{1,0:T(4,128)}, u32[]{:S(2)}) copy-start(f32[3,1024]{1,0:T(4,128)} %copy-done.15) | copy-start | bytes 36868
  516.7 11.7 %copy-start.18 = (f32[3,1024]{1,0:T(4,128)S(1)}, f32[3,1024]{1,0:T(4,128)}, u32[]{:S(2)}) copy-start(f32[3,1024]{1,0:T(4,128)} %copy-done.17) | copy-start | bytes 36868
  516.7 11.7 %copy-start.20 = (f32[3,1024]{1,0:T(4,128)S(1)}, f32[3,1024]{1,0:T(4,128)}, u32[]{:S(2)}) copy-start(f32[3,1024]{1,0:T(4,128)} %copy-done.19) | copy-start | bytes 36868
  516.7 11.7 %copy-start.22 = (f32[3,1024]{1,0:T(4,128)S(1)}, f32[3,1024]{1,0:T(4,128)}, u32[]{:S(2)}) copy-start(f32[3,1024]{1,0:T(4,128)} %copy-done.21) | copy-start | bytes 36868
  516.7 11.7 %copy-start.24 = (f32[3,1024]{1,0:T(4,128)S(1)}, f32[3,1024]{1,0:T(4,128)}, u32[]{:S(2)}) copy-start(f32[3,1024]{1,0:T(4,128)} %copy-done.23) | copy-start | bytes 36868
  516.7 11.7 %copy-start.26 = (f32[3,1,1024]{2,0,1:T(4,128)S(1)}, f32[3,1,1024]{2,0,1:T(4,128)}, u32[]{:S(2)}) copy-start(f32[3,1,1024]{2,0,1:T(4,128)} %copy-done.25) | copy-start | bytes 36868
  516.7 6.1 %collective-permute-start.1 = (f32[3,6,1024]{2,1,0:T(8,128)S(1)}, f32[3,6,1024]{2,1,0:T(8,128)S(1)}, u32[]{:S(2)}, u32[]{:S(2)}) collective-permute-start(f32[3,6,1024]{2,1,0:T(8,128)S(1)} %slice.142), channel_id=1, source_target_pairs={{8,0},{16,8},{24,16},{9,1},{17,9},{25,17},{10,2},{18,10},{26,18},{... | collective-permute-start | bytes 221192 | tf_op jit(solution)/shard_map/ppermute | solution.py:29
Sparse Core Ops, SparseCore 0:
  10.2 229.2 all-gather.4
where the time goes:
time: 584 us; the launch traced here: 573 us
  local copies, waits for them, and re-layouts  203 us (35%)
  matrix products  190 us (33%)
  other arithmetic  136 us (23%)
  blocking collectives  16.9 us (3%)
  between operations  15.1 us (3%)
  starting transfers between devices  6.78 us (1%)
    dot_general x1, matrix products, shards(): jnp.einsum('cij,njc->nic', toeplitz_mat, u_blocks, precision=HIGHEST)  57.3 us
    rev x1, local copies, waits for them, and re-layouts, toeplitz_rows(): return hankel[:, ::-1, :]  43.2 us
    unnamed x79, local copies, waits for them, and re-layouts  42.1 us
    add x1, other arithmetic, shards(): filtered + short_taps[:, tap_index, None, :] * extended[:, begin:begin +...  35.5 us
    another operation x2, local copies, waits for them, and re-layouts, toeplitz_rows(): repeated = jnp.tile(flipped, (1, block + 1))[:, :block * 2 * block]  35.2 us
    dot_general x1, matrix products, shards(): jnp.einsum('cij,nic->njc', toeplitz_mat, grad_blocks, precision=HIGHEST)  33.9 us
    another operation x1, other arithmetic  31.3 us
    dot_general x1, matrix products, shards(): lax.dot_general(lax.all_gather(grad_out, 'tp', axis=1, tiled=True), out_w...  27.4 us
  transfers between devices with their start and end apart: 3, of which 1 were waited for; matrix products, arithmetic and copies ran while one was open for 43% of the time, Pallas kernels for 0%

commit v1 on v0

v1 whole, which is shorter than its diff:
```python
import jax
import jax.numpy as jnp
from jax import lax
from jax.experimental import pallas as pl
from jax.experimental.pallas import tpu as pltpu
from jax.sharding import PartitionSpec as P

LANES = 128
SEGS = 8
UNROLL = 8
HALO = 16
CHUNKS = 4
MESH = pl.DeviceIdType.MESH
F32 = jnp.float32


def from_behind(block, axis, distance):
    devices = range(lax.axis_size(axis))
    route = [(i - distance, i) for i in devices if i - distance in devices]
    return lax.ppermute(block, axis, route)


def power(base, exponent):
    result = None
    while exponent:
        if exponent & 1:
            result = base if result is None else result * base
        exponent >>= 1
        if exponent:
            base = base * base
    return result


def spread(row):
    return jnp.broadcast_to(row, (SEGS, LANES))


def tree_sum(terms):
    while len(terms) > 1:
        paired = [a + b for a, b in zip(terms[::2], terms[1::2])]
        terms = paired + ([terms[-1]] if len(terms) % 2 else [])
    return terms[0]


def short_pass(load, store, taps, steps, history):
    def body(outer, past):
        past = list(past)
        for inner in range(UNROLL):
            step = outer * UNROLL + inner
            past = [load(step)] + past
            store(step, tree_sum([tap * row for tap, row in zip(taps, past)]))
            past = past[: len(taps) - 1]
        return tuple(past)

    lax.fori_loop(0, steps // UNROLL, body, tuple(history))


def forward_ends(
    q_ref, k_ref, v_ref, prior_ref, taps_ref, poles_ref,
    qs_ref, ks_ref, vs_ref, ends_ref, own_ref, wide,
):
    steps, tok_rows = qs_ref.shape[0], q_ref.shape[0]
    modes, tap_count = poles_ref.shape[0], taps_ref.shape[1]
    for which, (source, target) in enumerate(((q_ref, qs_ref), (k_ref, ks_ref), (v_ref, vs_ref))):
        wide[0:HALO, :] = prior_ref[which].astype(F32)
        wide[HALO : HALO + tok_rows, :] = source[...].astype(F32)
        taps = [spread(taps_ref[which, j : j + 1, :]) for j in range(tap_count)]

        def load(step):
            return wide[pl.ds(HALO + step, SEGS, stride=steps), :]

        def store(step, value, target=target):
            target[step] = value

        short_pass(load, store, taps, steps, [load(-1 - j) for j in range(tap_count - 1)])
    poles = [spread(poles_ref[m : m + 1, :]) for m in range(modes)]

    def body(outer, states):
        for inner in range(UNROLL):
            step = outer * UNROLL + inner
            row = ks_ref[step] * vs_ref[step]
            states = tuple(p * s + row for p, s in zip(poles, states))
        return states

    zero = jnp.zeros((SEGS, LANES), F32)
    states = lax.fori_loop(0, steps // UNROLL, body, (zero,) * modes)
    for m in range(modes):
        ends_ref[m] = states[m]
    seg_decay = power(poles_ref[...], steps)
    run = ends_ref[:, 0, :]
    for seg in range(1, SEGS):
        run = seg_decay * run + ends_ref[:, seg, :]
    own_ref[...] = run


def entering(mine, gathered_ref, ends_ref, poles_ref, starts, steps, backward):
    count = gathered_ref.shape[0]
    seg_decay = power(poles_ref[...], steps)
    block_decay = power(seg_decay, SEGS)
    run = jnp.zeros_like(seg_decay)
    order = range(count)
    for k in reversed(order) if backward else order:
        keep = (k > mine) if backward else (k < mine)
        run = jnp.where(keep, block_decay * run + gathered_ref[k], run)
    segs = range(SEGS)
    for seg in reversed(segs) if backward else segs:
        starts[:, seg, :] = run
        run = seg_decay * run + ends_ref[:, seg, :]


def forward_out(
    mine, ks_ref, vs_ref, ends_ref, gathered_ref, poles_ref, residues_ref, long_ref, starts,
):
    steps = ks_ref.shape[0]
    modes = poles_ref.shape[0]
    entering(mine, gathered_ref, ends_ref, poles_ref, starts, steps, False)
    poles = [spread(poles_ref[m : m + 1, :]) for m in range(modes)]
    residues = [spread(residues_ref[m : m + 1, :]) for m in range(modes)]

    def body(outer, states):
        for inner in range(UNROLL):
            step = outer * UNROLL + inner
            row = ks_ref[step] * vs_ref[step]
            states = tuple(p * s + row for p, s in zip(poles, states))
            out = tree_sum([r * s for r, s in zip(residues, states)])
            long_ref[step] = out
        return states

    lax.fori_loop(0, steps // UNROLL, body, tuple(starts[m] for m in range(modes)))


def backward_ends(mixed_ref, qs_ref, poles_ref, ends_ref, own_ref, wide):
    steps, tok_rows = qs_ref.shape[0], mixed_ref.shape[0]
    modes = poles_ref.shape[0]
    poles = [spread(poles_ref[m : m + 1, :]) for m in range(modes)]
    wide[0:tok_rows, :] = mixed_ref[...]

    def body(outer, states):
        for inner in range(UNROLL):
            step = steps - 1 - (outer * UNROLL + inner)
            row = wide[pl.ds(step, SEGS, stride=steps), :] * qs_ref[step]
            states = tuple(p * s + row for p, s in zip(poles, states))
        return states

    zero = jnp.zeros((SEGS, LANES), F32)
    states = lax.fori_loop(0, steps // UNROLL, body, (zero,) * modes)
    for m in range(modes):
        ends_ref[m] = states[m]
    seg_decay = power(poles_ref[...], steps)
    run = ends_ref[:, SEGS - 1, :]
    for seg in reversed(range(SEGS - 1)):
        run = seg_decay * run + ends_ref[:, seg, :]
    own_ref[...] = run


def backward_out(
    mine_ref, mixed_ref, qs_ref, ks_ref, vs_ref, long_ref, ends_ref, gathered_ref,
    taps_ref, poles_ref, residues_ref,
    gated_ref, gq_ref, gk_ref, gv_ref, heads_ref, tails_ref, starts, grads, wide,
):
    steps, tok_rows = qs_ref.shape[0], mixed_ref.shape[0]
    modes, tap_count = poles_ref.shape[0], taps_ref.shape[1]
    rim = tap_count - 1
    entering(mine_ref[0], gathered_ref, ends_ref, poles_ref, starts, steps, True)
    poles = [spread(poles_ref[m : m + 1, :]) for m in range(modes)]
    residues = [spread(residues_ref[m : m + 1, :]) for m in range(modes)]

    def body(outer, states):
        for inner in range(UNROLL):
            step = steps - 1 - (outer * UNROLL + inner)
            mixed = mixed_ref[pl.ds(step, SEGS, stride=steps), :]
            q_row, long_row = qs_ref[step], long_ref[step]
            row = mixed * q_row
            states = tuple(p * s + row for p, s in zip(poles, states))
            out = tree_sum([r * s for r, s in zip(residues, states)])
            grads[0, step] = mixed * long_row
            wide[pl.ds(step, SEGS, stride=steps), :] = q_row * long_row
            grads[1, step] = out * vs_ref[step]
            grads[2, step] = out * ks_ref[step]
        return states

    lax.fori_loop(0, steps // UNROLL, body, tuple(starts[m] for m in range(modes)))
    gated_ref[...] = wide[...].astype(jnp.bfloat16)
    zero_row = jnp.zeros((1, LANES), F32)
    for which, target in enumerate((gq_ref, gk_ref, gv_ref)):
        heads_ref[which] = grads[which, 0:8, 0, :]
        later = [
            jnp.concatenate([grads[which, j][1:], zero_row], axis=0) for j in range(rim)
        ]
        taps = [spread(taps_ref[which, j : j + 1, :]) for j in range(tap_count)]

        def load(step, which=which):
            return grads[which, steps - 1 - step]

        def store(step, value):
            wide[pl.ds(steps - 1 - step, SEGS, stride=steps), :] = value

        short_pass(load, store, taps, steps, later)
        tails_ref[which] = wide[tok_rows - 8 :, :]
        target[...] = wide[...].astype(jnp.bfloat16)


def own_plane(tp):
    z, x = tp // 2, tp % 2
    low = z < 2
    place = jnp.where(low, z, 3 - z)

    def shard(p, column):
        return jnp.where(low, p, 3 - p) * 2 + column

    return place, x, shard


def gather_and_multiply(
    grad_ref, weight_ref, q_ref, k_ref, v_ref, taps_ref, poles_ref, residues_ref,
    mixed_ref, qs_ref, ks_ref, vs_ref, long_ref, back_ref, gathered_back_ref,
    got, tiles, halo, wide, ends, own, gathered, starts,
    send_sem, recv_sem, tile_sem, mine_sem, halo_send, halo_recv, state_send, state_recv,
):
    count = lax.axis_size("ctx")
    mine = lax.axis_index("ctx")
    tp = lax.axis_index("tp")
    place, x, shard = own_plane(tp)
    is_end = place == 0
    is_mid = place == 1
    tok_rows, chan = mixed_ref.shape
    feat = grad_ref.shape[1]
    part = tok_rows // CHUNKS
    half = CHUNKS // 2
    inward, outward, across = shard(place + 1, x), shard(place - 1, x), shard(place, 1 - x)

    barrier = pltpu.get_barrier_semaphore()
    greeted = jnp.where(is_end, shard(3, x), outward)
    for peer in (inward, across, greeted):
        pl.semaphore_signal(barrier, inc=1, device_id={"tp": peer}, device_id_type=MESH)
    for gap in range(1, count):
        other = lax.rem(mine + gap, count)
        pl.semaphore_signal(barrier, inc=1, device_id={"ctx": other}, device_id_type=MESH)
    pl.semaphore_wait(barrier, count + 2)

    def rows(c):
        return pl.ds(pl.multiple_of(c * part, part), part)

    def copy(slot, c, way, source=None):
        piece = got.at[slot, rows(c), :]
        return pltpu.make_async_remote_copy(
            src_ref=piece if source is None else source.at[rows(c), :],
            dst_ref=piece,
            send_sem=send_sem.at[way, slot, c],
            recv_sem=recv_sem.at[slot, c],
            device_id={"tp": (inward, outward, across)[way]},
            device_id_type=MESH,
        )

    def tile(slot, buffer):
        columns = pl.ds(pl.multiple_of(slot * feat, feat), feat)
        return pltpu.make_async_copy(
            weight_ref.at[:, columns], tiles.at[buffer], tile_sem.at[buffer]
        )

    def halo_copy(which):
        source = (q_ref, k_ref, v_ref)[which]
        return pltpu.make_async_remote_copy(
            src_ref=source.at[pl.ds(tok_rows - HALO, HALO), :],
            dst_ref=halo.at[which],
            send_sem=halo_send.at[which],
            recv_sem=halo_recv.at[which],
            device_id={"ctx": lax.rem(mine + 1, count)},
            device_id_type=MESH,
        )

    def state_copy(gap, way, landing):
        return pltpu.make_async_remote_copy(
            src_ref=own.at[way],
            dst_ref=landing.at[mine],
            send_sem=state_send.at[way, gap],
            recv_sem=state_recv.at[way, gap],
            device_id={"ctx": lax.rem(mine + gap, count)},
            device_id_type=MESH,
        )

    def state_exchange(way, landing):
        landing[mine] = own[way]
        for gap in range(1, count):
            state_copy(gap, way, landing).start()

    def state_wait(way, landing):
        for gap in range(1, count):
            state_copy(gap, way, landing).wait()

    def pair(k, end_slot, mid_slot):
        return jnp.where(is_end, end_slot, mid_slot)

    order = (
        tp,
        shard(place + 1, x),
        pair(2, shard(0, 1 - x), shard(0, x)),
        shard(place + 2, x),
        pair(4, shard(3, x), shard(1, 1 - x)),
        pair(5, shard(2, 1 - x), shard(0, 1 - x)),
        pair(6, shard(1, 1 - x), shard(2, 1 - x)),
        shard(3, 1 - x),
    )

    def pick(k):
        slot = order[7]
        for i in range(7):
            slot = jnp.where(k == i, order[i], slot)
        return slot

    for c in range(CHUNKS):
        for way in (0, 2):
            copy(tp, c, way, grad_ref).start()

        @pl.when(is_mid)
        def _():
            copy(tp, c, 1, grad_ref).start()

    @pl.when(mine < count - 1)
    def _():
        for which in range(3):
            halo_copy(which).start()

    mine_copy = pltpu.make_async_copy(grad_ref, got.at[tp], mine_sem)
    mine_copy.start()
    tile(tp, 0).start()

    @pl.when(mine == 0)
    def _():
        halo[...] = jnp.zeros_like(halo)

    @pl.when(mine > 0)
    def _():
        for which in range(3):
            halo_copy(which).wait_recv()

    groups = chan // LANES
    share = groups // CHUNKS

    def lanes(g):
        return pl.ds(pl.multiple_of(g * LANES, LANES), LANES)

    def first_part(c, carry):
        @pl.loop(0, share)
        def _(u):
            at = lanes(c * share + u)
            forward_ends(
                q_ref.at[:, at], k_ref.at[:, at], v_ref.at[:, at], halo.at[:, :, at],
                taps_ref.at[:, :, at], poles_ref.at[:, at], qs_ref.at[:, :, at],
                ks_ref.at[:, :, at], vs_ref.at[:, :, at], ends.at[:, :, at],
                own.at[0, :, at], wide,
            )

        copy(order[1], c, 0).wait_recv()

        @pl.when(is_mid | (c < half))
        def _():
            copy(order[1], c, 2).start()

        @pl.when(is_mid)
        def _():
            copy(order[1], c, 1).start()

        copy(order[2], c, 0).wait_recv()
        copy(order[2], c, 0).start()
        return carry

    lax.fori_loop(0, CHUNKS, first_part, 0)
    state_exchange(0, gathered)
    state_wait(0, gathered)

    def second_part(c, carry):
        @pl.loop(0, share)
        def _(u):
            at = lanes(c * share + u)
            forward_out(
                mine, ks_ref.at[:, :, at], vs_ref.at[:, :, at], ends.at[:, :, at],
                gathered.at[:, :, at], poles_ref.at[:, at], residues_ref.at[:, at],
                long_ref.at[:, :, at], starts,
            )

        copy(order[3], c, 0).wait_recv()
        copy(order[3], c, 2).start()

        @pl.when(is_mid)
        def _():
            copy(order[3], c, 1).start()

        return carry

    lax.fori_loop(0, CHUNKS, second_part, 0)
    mine_copy.wait()

    def multiply(k, carry):
        slot = pick(k)

        @pl.when(k == 4)
        def _():
            for c in range(CHUNKS):
                copy(order[4], c, 0).wait_recv()

                @pl.when(is_end)
                def _():
                    copy(order[4], c, 2).start()

                if c >= half:

                    @pl.when(is_mid)
                    def _():
                        copy(order[4], c, 1).start()

        @pl.when(k > 4)
        def _():
            for c in range(CHUNKS):
                copy(slot, c, 0).wait_recv()

        buffer = k % 2
        tile(slot, buffer).wait()

        @pl.when(k < 7)
        def _():
            tile(pick(k + 1), 1 - buffer).start()

        @pl.loop(0, chan // 256)
        def _(n):
            at = pl.ds(pl.multiple_of(n * 256, 256), 256)
            term = lax.dot_general(
                got[slot], tiles[buffer, at, :], (((1,), (1,)), ((), ())),
                preferred_element_type=F32,
            )

            @pl.when(k == 0)
            def _():
                mixed_ref[:, at] = term

            @pl.when(k > 0)
            def _():
                mixed_ref[:, at] += term

        return carry

    lax.fori_loop(0, 8, multiply, 0)

    @pl.loop(0, groups)
    def _(g):
        at = lanes(g)
        backward_ends(
            mixed_ref.at[:, at], qs_ref.at[:, :, at], poles_ref.at[:, at], back_ref.at[:, :, at],
            own.at[1, :, at], wide,
        )

    state_exchange(1, gathered_back_ref)
    for c in range(CHUNKS):
        copy(tp, c, 0, grad_ref).wait_send()
        copy(tp, c, 2, grad_ref).wait_send()
        copy(order[2], c, 0).wait_send()
        copy(order[3], c, 2).wait_send()

        @pl.when(is_mid | (c < half))
        def _():
            copy(order[1], c, 2).wait_send()

        @pl.when(is_end)
        def _():
            copy(order[4], c, 2).wait_send()

        @pl.when(is_mid)
        def _():
            copy(tp, c, 1, grad_ref).wait_send()
            copy(order[1], c, 1).wait_send()
            copy(order[3], c, 1).wait_send()
            if c >= half:
                copy(order[4], c, 1).wait_send()

    @pl.when(mine < count - 1)
    def _():
        for which in range(3):
            halo_copy(which).wait_send()

    state_wait(1, gathered_back_ref)


def lanes_spec(shape):
    lead = len(shape) - 1
    return pl.BlockSpec(tuple(shape[:-1]) + (LANES,), lambda g: (0,) * lead + (g,))


def call(body, inputs, outputs, scratch, flops, name, scalars=0):
    moved = sum(x.size * x.dtype.itemsize for x in list(inputs) + list(outputs))
    return pl.pallas_call(
        body,
        grid=(outputs[0].shape[-1] // LANES,),
        in_specs=[pl.BlockSpec(memory_space=pltpu.SMEM)] * scalars
        + [lanes_spec(x.shape) for x in inputs[scalars:]],
        out_specs=[lanes_spec(x.shape) for x in outputs],
        out_shape=list(outputs),
        scratch_shapes=scratch,
        cost_estimate=pl.CostEstimate(flops=flops, bytes_accessed=moved, transcendentals=0),
        compiler_params=pltpu.CompilerParams(vmem_limit_bytes=32 * 1024 * 1024),
        name=name,
    )(*inputs)


def shards(
    query_in, key_in, value_in, short_taps, modal_poles, modal_residues, out_weight, grad_out
):
    tap_count = short_taps.shape[1]
    rim = tap_count - 1
    tok_rows, chan = query_in.shape
    modes = modal_poles.shape[0]
    steps = tok_rows // SEGS
    mine = lax.axis_index("ctx").astype(jnp.int32)[None]
    sds = jax.ShapeDtypeStruct
    seg_shape = sds((steps, SEGS, chan), F32)
    state_shape = sds((modes, SEGS, chan), F32)
    own_shape = sds((modes, chan), F32)
    plain = sds((tok_rows, chan), jnp.bfloat16)
    rows_shape = sds((3, 8, chan), F32)
    work = tok_rows * chan
    count = lax.axis_size("ctx")
    if lax.axis_size("tp") == 8 and chan % (LANES * CHUNKS) == 0 and chan == grad_out.shape[1]:
        outputs = (
            sds((tok_rows, chan), F32), seg_shape, seg_shape, seg_shape, seg_shape, state_shape,
            sds((count, modes, chan), F32),
        )
        vmem = pl.BlockSpec(memory_space=pltpu.VMEM)
        hbm = pl.BlockSpec(memory_space=pl.ANY)
        dma = pltpu.SemaphoreType.DMA
        mixed, qs, ks, vs, long_out, ends, gathered = pl.pallas_call(
            gather_and_multiply,
            out_shape=outputs,
            in_specs=[hbm, hbm] + [vmem] * 6,
            out_specs=[vmem] * len(outputs),
            scratch_shapes=[
                pltpu.VMEM((8, tok_rows, grad_out.shape[1]), jnp.bfloat16),
                pltpu.VMEM((2, chan, grad_out.shape[1]), jnp.bfloat16),
                pltpu.VMEM((3, HALO, chan), jnp.bfloat16),
                pltpu.VMEM((tok_rows + HALO, LANES), F32),
                pltpu.VMEM((modes, SEGS, chan), F32),
                pltpu.VMEM((2, modes, chan), F32),
                pltpu.VMEM((count, modes, chan), F32),
                pltpu.VMEM((modes, SEGS, LANES), F32),
                dma((3, 8, CHUNKS)),
                dma((8, CHUNKS)),
                dma((2,)),
                dma,
                dma((3,)),
                dma((3,)),
                dma((2, count)),
                dma((2, count)),
            ],
            cost_estimate=pl.CostEstimate(
                flops=2 * work * out_weight.shape[1],
                bytes_accessed=2 * out_weight.size,
                transcendentals=0,
            ),
            compiler_params=pltpu.CompilerParams(
                collective_id=0, has_side_effects=True, vmem_limit_bytes=58 * 1024 * 1024
            ),
            name="gather_and_multiply",
        )(grad_out, out_weight, query_in, key_in, value_in, short_taps, modal_poles, modal_residues)
    else:
        gathered_out = lax.all_gather(grad_out, "tp", axis=1, tiled=True)
        last = jnp.stack([x[tok_rows - rim :] for x in (query_in, key_in, value_in)])
        prior = from_behind(last, "ctx", 1)
        prior = jnp.pad(prior, ((0, 0), (HALO - rim, 0), (0, 0)))
        qs, ks, vs, ends, own = call(
            forward_ends,
            (query_in, key_in, value_in, prior, short_taps, modal_poles),
            (seg_shape, seg_shape, seg_shape, state_shape, own_shape),
            [pltpu.VMEM((tok_rows + HALO, LANES), F32)],
            work * (3 * 2 * tap_count + 2 * modes),
            "forward_ends",
        )
        (long_out,) = call(
            lambda mine_ref, *refs: forward_out(mine_ref[0], *refs),
            (mine, ks, vs, ends, lax.all_gather(own, "ctx"), modal_poles, modal_residues),
            (seg_shape,),
            [pltpu.VMEM((modes, SEGS, LANES), F32)],
            work * 4 * modes,
            "forward_out",
            1,
        )
        mixed = lax.dot_general(
            gathered_out, out_weight, (((1,), (1,)), ((), ())), preferred_element_type=F32
        )
        ends, own = call(
            backward_ends,
            (mixed, qs, modal_poles),
            (state_shape, own_shape),
            [pltpu.VMEM((tok_rows, LANES), F32)],
            work * 2 * modes,
            "backward_ends",
        )
        gathered = lax.all_gather(own, "ctx")
    gated, gq, gk, gv, heads, tails = call(
        backward_out,
        (mine, mixed, qs, ks, vs, long_out, ends, gathered, short_taps,
         modal_poles, modal_residues),
        (plain, plain, plain, plain, rows_shape, rows_shape),
        [
            pltpu.VMEM((modes, SEGS, LANES), F32),
            pltpu.VMEM((3, steps, SEGS, LANES), F32),
            pltpu.VMEM((tok_rows, LANES), F32),
        ],
        work * (4 * modes + 6 * tap_count),
        "backward_out",
        1,
    )
    later = from_behind(heads, "ctx", -1)
    for j in range(1, tap_count):
        tails = tails.at[:, 8 - j :, :].add(short_taps[:, j, None, :] * later[:, :j, :])
    tails = tails.astype(jnp.bfloat16)
    grads = [
        lax.dynamic_update_slice(g, tails[i], (tok_rows - 8, 0)) for i, g in enumerate((gq, gk, gv))
    ]
    return (gated, *grads)


def solution(mesh):
    placed = (
        P("ctx", "tp"),
        P("ctx", "tp"),
        P("ctx", "tp"),
        P(None, None, "tp"),
        P(None, "tp"),
        P(None, "tp"),
        P("tp", None),
        P("ctx", "tp"),
    )
    return jax.shard_map(
        shards,
        mesh=mesh,
        in_specs=placed,
        out_specs=(P("ctx", "tp"), P("ctx", "tp"), P("ctx", "tp"), P("ctx", "tp")),
        check_vma=False,
    )
```

time: 584 us -> 248 us (0.42); the launches traced: 573 us -> 248 us
  Pallas kernels: 0 us -> 226 us
  matrix products: 190 us -> 0 us
  local copies, waits for them, and re-layouts: 203 us -> 14.5 us
  other arithmetic: 136 us -> 0.2 us
  blocking collectives: 16.9 us -> 0 us
  between operations: 15.1 us -> 0.82 us
    pallas_call x0 -> x2, Pallas kernels: none -> 226 us  [the longest x1 193 us: shards(): pl.pallas_call(gather_and_multiply, out_shape=outputs, in_specs=[hbm, hbm...]
    dot_general x7 -> x0, matrix products: 190 us -> none  [the longest x1 57.3 us: shards(): jnp.einsum('cij,njc->nic', toeplitz_mat, u_blocks, precision=HIGHEST)]
    rev x5 -> x0, local copies, waits for them, and re-layouts: 57.3 us -> none  [the longest x1 43.2 us: toeplitz_rows(): return hankel[:, ::-1, :]]
    add x2 -> x3, other arithmetic: 36.1 us -> 0.06 us  [shards(): tails.at[:, 8 - j:, :].add(short_taps[:, j, None, :] * later[:, :j, :])]
    another operation x2 -> x0, local copies, waits for them, and re-layouts: 35.2 us -> none  [toeplitz_rows(): repeated = jnp.tile(flipped, (1, block + 1))[:, :block * 2 * block]]
    another operation x3 -> x0, other arithmetic: 33.4 us -> none
    unnamed x79 -> x23, local copies, waits for them, and re-layouts: 42.1 us -> 13 us
    mul x5 -> x0, other arithmetic: 21.3 us -> none  [the longest x1 7.49 us: shards(): grad_qs = grad_mixed * long_out]
  transfers between devices with their start and end apart: 3 -> 1, of which waited for: 1 -> 1; matrix products, arithmetic and copies ran while one was open for 43% -> 0% of each run, Pallas kernels for 0% -> 0%
where the time goes in v1:
time: 248 us
  Pallas kernels  226 us (91%)
  local copies, waits for them, and re-layouts  14.5 us (6%)
  waiting for transfers between devices  4.01 us (2%)
    pallas_call x1, Pallas kernels, shards(): pl.pallas_call(gather_and_multiply, out_shape=outputs, in_specs=[hbm, hbm...  193 us
    pallas_call x1, Pallas kernels, call(): pl.pallas_call(body, grid=(outputs[0].shape[-1] // LANES,), in_specs=[pl....  33.1 us
    unnamed x23, local copies, waits for them, and re-layouts  13 us
  transfers between devices with their start and end apart: 1, of which 1 were waited for; matrix products, arithmetic and copies ran while one was open for 0% of the time, Pallas kernels for 0%

profile of v1, /device:TPU:1, one launch (start us, length us, event | category | flops | bytes accessed | tf_op | source)
XLA Modules:
  0.0 247.7 jit_solution(3467177929546748116)
XLA Ops:
  0.6 0.0 copy-start.6
  0.6 0.0 copy-start.8
  0.7 0.0 copy-start.9
  0.7 193.2 %gather_and_multiply.1 = (f32[1024,1024]{1,0:T(8,128)}, f32[128,8,1024]{2,1,0:T(8,128)}, f32[128,8,1024]{2,1,0:T(8,128)}, f32[128,8,1024]{2,1,0:T(8,128)}, f32[1...) custom-call(bf16[1024,1024]{1,0:T(8,128)(2,1)} %grad_ref.1, bf16[1024,8192]{1,0:T(8,128)(2,1)} %weight_ref.1, ...), custom_call_target="tpu_custom_call" | custom-call | flops 17179869184 | bytes 16777216 | tf_op jit(solution)/shard_map/gather_and_multiply/pallas_call | solution.py:529
  193.9 0.0 copy-done.6
  193.9 0.0 copy-done.8
  193.9 0.0 copy-done.9
  193.9 0.0 copy-start
  193.9 2.2 copy-done
  196.1 0.0 copy-start.1
  196.1 2.2 copy-done.1
  198.3 0.0 copy-start.2
  198.3 2.2 copy-done.2
  200.5 0.0 copy-start.3
  200.5 2.2 copy-done.3
  202.7 0.0 copy-start.4
  202.7 2.2 copy-done.4
  204.9 0.0 copy-start.5
  204.9 1.0 copy-done.5
  205.9 0.0 copy-start.7
  205.9 0.9 copy-done.7
  206.9 33.1 %backward_out.1 = (bf16[1024,1024]{1,0:T(8,128)(2,1)}, bf16[1024,1024]{1,0:T(8,128)(2,1)}, bf16[1024,1024]{1,0:T(8,128)(2,1)}, bf16[1024,1024]{1,0:T(8,128)(2,1)...) custom-call(s32[1]{0:T(128)} %bitcast.mine_ref, f32[1024,1024]{1,0:T(8,128)S(1)} %copy-done, ...), custom_call_target="tpu_custom_call" | custom-call | flops 111149056 | bytes 30560260 | tf_op jit(solution)/shard_map/backward_out/pallas_call | solution.py:490
  240.0 1.9 collective-permute-start
  241.9 4.0 %collective-permute-done = f32[3,8,1024]{2,1,0:T(8,128)S(1)} collective-permute-done((f32[3,8,1024]{2,1,0:T(8,128)S(1)}, f32[3,8,1024]{2,1,0:T(8,128)S(1)}, u32[]{:S(2)}, u32[]{:S(2)}) %collective-permute-start) | collective-permute-done | bytes 98336 | tf_op jit(solution)/shard_map/ppermute | solution.py:20
  245.9 0.1 fusion.11
  246.0 0.1 scatter-add.20
  246.2 0.3 scatter-add.24
  246.6 0.2 scatter-add.26
  246.8 0.2 scatter-add.29
  247.1 0.6 fusion.7
  (9 shorter events, 0.2 us)
Async XLA Ops:
  0.6 193.3 %copy-start.6 = (f32[3,7,1024]{2,1,0:T(8,128)S(1)}, f32[3,7,1024]{2,1,0:T(8,128)}, u32[]{:S(2)}) copy-start(f32[3,7,1024]{2,1,0:T(8,128)} %taps_ref.3) | copy-start | bytes 258052
  0.6 193.3 %copy-start.8 = (f32[16,1024]{1,0:T(8,128)S(1)}, f32[16,1024]{1,0:T(8,128)}, u32[]{:S(2)}) copy-start(f32[16,1024]{1,0:T(8,128)} %poles_ref.3) | copy-start | bytes 196612
  0.7 193.3 %copy-start.9 = (f32[16,1024]{1,0:T(8,128)S(1)}, f32[16,1024]{1,0:T(8,128)}, u32[]{:S(2)}) copy-start(f32[16,1024]{1,0:T(8,128)} %residues_ref.3) | copy-start | bytes 196612
  193.9 2.2 copy-start
  196.1 2.2 copy-start.1
  198.3 2.2 copy-start.2
  200.5 2.2 copy-start.3
  202.7 2.2 copy-start.4
  204.9 1.0 copy-start.5
  205.9 0.9 copy-start.7
  240.0 5.9 %collective-permute-start = (f32[3,8,1024]{2,1,0:T(8,128)S(1)}, f32[3,8,1024]{2,1,0:T(8,128)S(1)}, u32[]{:S(2)}, u32[]{:S(2)}) collective-permute-start(f32[3,8,1024]{2,1,0:T(8,128)S(1)} %get-tuple-element.99), channel_id=1, source_target_pairs={{8,0},{16,8},{24,16},{9,1},{17,9},{25,17},{10,2},{18,10},{26,18},{... | collective-permute-start | bytes 294920 | tf_op jit(solution)/shard_map/ppermute | solution.py:20

commit v2 on v1

--- a/solution.py
+++ b/solution.py
@@ -129,68 +129,85 @@
     lax.fori_loop(0, steps // UNROLL, body, tuple(starts[m] for m in range(modes)))
 
 
-def backward_ends(mixed_ref, qs_ref, poles_ref, ends_ref, own_ref, wide):
-    steps, tok_rows = qs_ref.shape[0], mixed_ref.shape[0]
+def backward_zero(
+    base, mixed_ref, qs_ref, long_ref, poles_ref, residues_ref, states_ref, gq_ref, gp_ref,
+):
+    part = mixed_ref.shape[0] // SEGS
     modes = poles_ref.shape[0]
     poles = [spread(poles_ref[m : m + 1, :]) for m in range(modes)]
-    wide[0:tok_rows, :] = mixed_ref[...]
+    residues = [spread(residues_ref[m : m + 1, :]) for m in range(modes)]
 
     def body(outer, states):
         for inner in range(UNROLL):
-            step = steps - 1 - (outer * UNROLL + inner)
-            row = wide[pl.ds(step, SEGS, stride=steps), :] * qs_ref[step]
+            place = part - 1 - (outer * UNROLL + inner)
+            step = base + place
+            mixed = mixed_ref[pl.ds(place, SEGS, stride=part), :]
+            row = mixed * qs_ref[step]
             states = tuple(p * s + row for p, s in zip(poles, states))
+            gq_ref[step] = mixed * long_ref[step]
+            gp_ref[step] = tree_sum([r * s for r, s in zip(residues, states)])
         return states
 
-    zero = jnp.zeros((SEGS, LANES), F32)
-    states = lax.fori_loop(0, steps // UNROLL, body, (zero,) * modes)
+    states = lax.fori_loop(
+        0, part // UNROLL, body, tuple(states_ref[m] for m in range(modes))
+    )
     for m in range(modes):
-        ends_ref[m] = states[m]
+        states_ref[m] = states[m]
+
+
+def backward_own(ends_ref, poles_ref, steps):
     seg_decay = power(poles_ref[...], steps)
     run = ends_ref[:, SEGS - 1, :]
     for seg in reversed(range(SEGS - 1)):
         run = seg_decay * run + ends_ref[:, seg, :]
-    own_ref[...] = run
+    return run
+
+
+def backward_whole(
+    mixed_ref, qs_ref, long_ref, poles_ref, residues_ref, ends_ref, gq_ref, gp_ref, own_ref
+):
+    ends_ref[...] = jnp.zeros_like(ends_ref)
+    backward_zero(
+        0, mixed_ref, qs_ref, long_ref, poles_ref, residues_ref, ends_ref, gq_ref, gp_ref
+    )
+    own_ref[...] = backward_own(ends_ref, poles_ref, qs_ref.shape[0])
 
 
 def backward_out(
-    mine_ref, mixed_ref, qs_ref, ks_ref, vs_ref, long_ref, ends_ref, gathered_ref,
+    mine_ref, grad_q_ref, grad_p_ref, qs_ref, ks_ref, vs_ref, long_ref, ends_ref, gathered_ref,
     taps_ref, poles_ref, residues_ref,
     gated_ref, gq_ref, gk_ref, gv_ref, heads_ref, tails_ref, starts, grads, wide,
 ):
-    steps, tok_rows = qs_ref.shape[0], mixed_ref.shape[0]
+    steps, tok_rows = qs_ref.shape[0], gq_ref.shape[0]
     modes, tap_count = poles_ref.shape[0], taps_ref.shape[1]
     rim = tap_count - 1
     entering(mine_ref[0], gathered_ref, ends_ref, poles_ref, starts, steps, True)
     poles = [spread(poles_ref[m : m + 1, :]) for m in range(modes)]
-    residues = [spread(residues_ref[m : m + 1, :]) for m in range(modes)]
-
-    def body(outer, states):
+
+    def body(outer, shares):
         for inner in range(UNROLL):
             step = steps - 1 - (outer * UNROLL + inner)
-            mixed = mixed_ref[pl.ds(step, SEGS, stride=steps), :]
-            q_row, long_row = qs_ref[step], long_ref[step]
-            row = mixed * q_row
-            states = tuple(p * s + row for p, s in zip(poles, states))
-            out = tree_sum([r * s for r, s in zip(residues, states)])
-            grads[0, step] = mixed * long_row
-            wide[pl.ds(step, SEGS, stride=steps), :] = q_row * long_row
-            grads[1, step] = out * vs_ref[step]
-            grads[2, step] = out * ks_ref[step]
-        return states
-
-    lax.fori_loop(0, steps // UNROLL, body, tuple(starts[m] for m in range(modes)))
+            shares = tuple(p * s for p, s in zip(poles, shares))
+            out = grad_p_ref[step] + tree_sum(list(shares))
+            grads[0, step] = out * vs_ref[step]
+            grads[1, step] = out * ks_ref[step]
+            wide[pl.ds(step, SEGS, stride=steps), :] = qs_ref[step] * long_ref[step]
+        return shares
+
+    lax.fori_loop(
+        0, steps // UNROLL, body,
+        tuple(spread(residues_ref[m : m + 1, :]) * starts[m] for m in range(modes)),
+    )
     gated_ref[...] = wide[...].astype(jnp.bfloat16)
     zero_row = jnp.zeros((1, LANES), F32)
-    for which, target in enumerate((gq_ref, gk_ref, gv_ref)):
-        heads_ref[which] = grads[which, 0:8, 0, :]
-        later = [
-            jnp.concatenate([grads[which, j][1:], zero_row], axis=0) for j in range(rim)
-        ]
+    sources = (grad_q_ref, grads.at[0], grads.at[1])
+    for which, (source, target) in enumerate(zip(sources, (gq_ref, gk_ref, gv_ref))):
+        heads_ref[which] = source[0:8, 0, :]
+        later = [jnp.concatenate([source[j][1:], zero_row], axis=0) for j in range(rim)]
         taps = [spread(taps_ref[which, j : j + 1, :]) for j in range(tap_count)]
 
-        def load(step, which=which):
-            return grads[which, steps - 1 - step]
+        def load(step, source=source):
+            return source[steps - 1 - step]
 
         def store(step, value):
             wide[pl.ds(steps - 1 - step, SEGS, stride=steps), :] = value
@@ -212,10 +229,10 @@
 
 
 def gather_and_multiply(
-    grad_ref, weight_ref, q_ref, k_ref, v_ref, taps_ref, poles_ref, residues_ref,
-    mixed_ref, qs_ref, ks_ref, vs_ref, long_ref, back_ref, gathered_back_ref,
-    got, tiles, halo, wide, ends, own, gathered, starts,
-    send_sem, recv_sem, tile_sem, mine_sem, halo_send, halo_recv, state_send, state_recv,
+    grad_ref, weight_ref, q_in, k_in, v_in, taps_ref, poles_ref, residues_ref,
+    gq_out, gp_out, qs_out, ks_out, vs_out, long_out, back_ref, gathered_back_ref,
+    q_ref, k_ref, v_ref, mixed_ref, qs_ref, ks_ref, vs_ref, long_ref, got, tiles, halo, wide, ends, own, gathered, starts,
+    send_sem, recv_sem, tile_sem, mine_sem, in_sem, out_sem, grad_sem, halo_send, halo_recv, state_send, state_recv,
 ):
     count = lax.axis_size("ctx")
     mine = lax.axis_index("ctx")
@@ -223,9 +240,9 @@
     place, x, shard = own_plane(tp)
     is_end = place == 0
     is_mid = place == 1
-    tok_rows, chan = mixed_ref.shape
-    feat = grad_ref.shape[1]
-    part = tok_rows // CHUNKS
+    tok_rows, chan = q_ref.shape
+    steps, feat = grad_ref.shape[1:]
+    part = steps // CHUNKS
     half = CHUNKS // 2
     inward, outward, across = shard(place + 1, x), shard(place - 1, x), shard(place, 1 - x)
 
@@ -239,12 +256,12 @@
     pl.semaphore_wait(barrier, count + 2)
 
     def rows(c):
-        return pl.ds(pl.multiple_of(c * part, part), part)
+        return pl.ds(pl.multiple_of((CHUNKS - 1 - c) * part, part), part)
 
     def copy(slot, c, way, source=None):
-        piece = got.at[slot, rows(c), :]
+        piece = got.at[slot, :, rows(c), :]
         return pltpu.make_async_remote_copy(
-            src_ref=piece if source is None else source.at[rows(c), :],
+            src_ref=piece if source is None else source.at[:, rows(c), :],
             dst_ref=piece,
             send_sem=send_sem.at[way, slot, c],
             recv_sem=recv_sem.at[slot, c],
@@ -259,7 +276,7 @@
         )
 
     def halo_copy(which):
-        source = (q_ref, k_ref, v_ref)[which]
+        source = (q_in, k_in, v_in)[which]
         return pltpu.make_async_remote_copy(
             src_ref=source.at[pl.ds(tok_rows - HALO, HALO), :],
             dst_ref=halo.at[which],
@@ -316,6 +333,21 @@
         def _():
             copy(tp, c, 1, grad_ref).start()
 
+    ins = [
+        pltpu.make_async_copy(source, target, in_sem.at[i])
+        for i, (source, target) in enumerate(((q_in, q_ref), (k_in, k_ref), (v_in, v_ref)))
+    ]
+    outs = [
+        pltpu.make_async_copy(source, target, out_sem.at[i])
+        for i, (source, target) in enumerate(
+            (
+                (qs_ref, qs_out), (ks_ref, ks_out), (vs_ref, vs_out), (long_ref, long_out),
+            )
+        )
+    ]
+    for each in ins:
+        each.start()
+
     @pl.when(mine < count - 1)
     def _():
         for which in range(3):
@@ -334,6 +366,8 @@
         for which in range(3):
             halo_copy(which).wait_recv()
 
+    for each in ins:
+        each.wait()
     groups = chan // LANES
     share = groups // CHUNKS
 
@@ -366,6 +400,8 @@
         return carry
 
     lax.fori_loop(0, CHUNKS, first_part, 0)
+    for each in outs[:3]:
+        each.start()
     state_exchange(0, gathered)
     state_wait(0, gathered)
 
@@ -389,7 +425,15 @@
         return carry
 
     lax.fori_loop(0, CHUNKS, second_part, 0)
+    outs[3].start()
     mine_copy.wait()
+
+    def product(slot, c, buffer):
+        term = lax.dot_general(
+            got[slot, :, rows(c), :].reshape(SEGS * part, feat), tiles[buffer],
+            (((1,), (1,)), ((), ())), preferred_element_type=F32,
+        )
+        return term.reshape(SEGS, part, chan)
 
     def multiply(k, carry):
         slot = pick(k)
@@ -409,46 +453,68 @@
                     def _():
                         copy(order[4], c, 1).start()
 
-        @pl.when(k > 4)
-        def _():
-            for c in range(CHUNKS):
-                copy(slot, c, 0).wait_recv()
-
         buffer = k % 2
         tile(slot, buffer).wait()
 
-        @pl.when(k < 7)
-        def _():
-            tile(pick(k + 1), 1 - buffer).start()
-
-        @pl.loop(0, chan // 256)
-        def _(n):
-            at = pl.ds(pl.multiple_of(n * 256, 256), 256)
-            term = lax.dot_general(
-                got[slot], tiles[buffer, at, :], (((1,), (1,)), ((), ())),
-                preferred_element_type=F32,
-            )
+        tile(pick(k + 1), 1 - buffer).start()
+
+        @pl.loop(0, CHUNKS)
+        def _(c):
+            @pl.when(k > 4)
+            def _():
+                copy(slot, c, 0).wait_recv()
+
+            at = rows(c)
+            term = product(slot, c, buffer)
 
             @pl.when(k == 0)
             def _():
-                mixed_ref[:, at] = term
+                mixed_ref[:, at, :] = term
 
             @pl.when(k > 0)
             def _():
-                mixed_ref[:, at] += term
+                mixed_ref[:, at, :] += term
 
         return carry
 
-    lax.fori_loop(0, 8, multiply, 0)
-
-    @pl.loop(0, groups)
-    def _(g):
-        at = lanes(g)
-        backward_ends(
-            mixed_ref.at[:, at], qs_ref.at[:, :, at], poles_ref.at[:, at], back_ref.at[:, :, at],
-            own.at[1, :, at], wide,
-        )
-
+    lax.fori_loop(0, 6, multiply, 0)
+    tile(order[7], 1).start()
+    for each in outs[1:3]:
+        each.wait()
+    gq_ref, gp_ref = ks_ref, vs_ref
+    back_ref[...] = jnp.zeros_like(back_ref)
+    tile(order[6], 0).wait()
+    tile(order[7], 1).wait()
+
+    def grad_copy(which, c):
+        source, target = ((gq_ref, gq_out), (gp_ref, gp_out))[which]
+        return pltpu.make_async_copy(
+            source.at[rows(c)], target.at[rows(c)], grad_sem.at[which, c]
+        )
+
+    def last_part(c, carry):
+        for i in (6, 7):
+            copy(order[i], c, 0).wait_recv()
+            mixed_ref[:, rows(c), :] += product(order[i], c, i - 6)
+        chunk = wide.at[0 : SEGS * part, :]
+
+        @pl.loop(0, groups)
+        def _(g):
+            at = lanes(g)
+            for seg in range(SEGS):
+                wide[seg * part : (seg + 1) * part, :] = mixed_ref[seg, rows(c), at]
+            backward_zero(
+                (CHUNKS - 1 - c) * part, chunk, qs_ref.at[:, :, at], long_ref.at[:, :, at],
+                poles_ref.at[:, at], residues_ref.at[:, at], back_ref.at[:, :, at],
+                gq_ref.at[:, :, at], gp_ref.at[:, :, at],
+            )
+
+        for which in range(2):
+            grad_copy(which, c).start()
+        return carry
+
+    lax.fori_loop(0, CHUNKS, last_part, 0)
+    own[1] = backward_own(back_ref, poles_ref, steps)
     state_exchange(1, gathered_back_ref)
     for c in range(CHUNKS):
         copy(tp, c, 0, grad_ref).wait_send()
@@ -478,6 +544,11 @@
             halo_copy(which).wait_send()
 
     state_wait(1, gathered_back_ref)
+    for each in (outs[0], outs[3]):
+        each.wait()
+    for which in range(2):
+        for c in range(CHUNKS):
+            grad_copy(which, c).wait()
 
 
 def lanes_spec(shape):
@@ -485,7 +556,7 @@
     return pl.BlockSpec(tuple(shape[:-1]) + (LANES,), lambda g: (0,) * lead + (g,))
 
 
-def call(body, inputs, outputs, scratch, flops, name, scalars=0):
+def call(body, inputs, outputs, scratch, flops, name, scalars=0, room=32):
     moved = sum(x.size * x.dtype.itemsize for x in list(inputs) + list(outputs))
     return pl.pallas_call(
         body,
@@ -496,7 +567,7 @@
         out_shape=list(outputs),
         scratch_shapes=scratch,
         cost_estimate=pl.CostEstimate(flops=flops, bytes_accessed=moved, transcendentals=0),
-        compiler_params=pltpu.CompilerParams(vmem_limit_bytes=32 * 1024 * 1024),
+        compiler_params=pltpu.CompilerParams(vmem_limit_bytes=room * 1024 * 1024),
         name=name,
     )(*inputs)
 
@@ -520,19 +591,22 @@
     count = lax.axis_size("ctx")
     if lax.axis_size("tp") == 8 and chan % (LANES * CHUNKS) == 0 and chan == grad_out.shape[1]:
         outputs = (
-            sds((tok_rows, chan), F32), seg_shape, seg_shape, seg_shape, seg_shape, state_shape,
+            seg_shape, seg_shape, seg_shape, seg_shape, seg_shape, seg_shape, state_shape,
             sds((count, modes, chan), F32),
         )
         vmem = pl.BlockSpec(memory_space=pltpu.VMEM)
         hbm = pl.BlockSpec(memory_space=pl.ANY)
         dma = pltpu.SemaphoreType.DMA
-        mixed, qs, ks, vs, long_out, ends, gathered = pl.pallas_call(
+        gq, gp, qs, ks, vs, long_out, ends, gathered = pl.pallas_call(
             gather_and_multiply,
             out_shape=outputs,
-            in_specs=[hbm, hbm] + [vmem] * 6,
-            out_specs=[vmem] * len(outputs),
-            scratch_shapes=[
-                pltpu.VMEM((8, tok_rows, grad_out.shape[1]), jnp.bfloat16),
+            in_specs=[hbm] * 5 + [vmem] * 3,
+            out_specs=[hbm] * 6 + [vmem] * 2,
+            scratch_shapes=[pltpu.VMEM((tok_rows, chan), jnp.bfloat16)] * 3
+            + [pltpu.VMEM((SEGS, steps, chan), F32)]
+            + [pltpu.VMEM(seg_shape.shape, F32)] * 4
+            + [
+                pltpu.VMEM((8, SEGS, steps, grad_out.shape[1]), jnp.bfloat16),
                 pltpu.VMEM((2, chan, grad_out.shape[1]), jnp.bfloat16),
                 pltpu.VMEM((3, HALO, chan), jnp.bfloat16),
                 pltpu.VMEM((tok_rows + HALO, LANES), F32),
@@ -544,6 +618,9 @@
                 dma((8, CHUNKS)),
                 dma((2,)),
                 dma,
+                dma((3,)),
+                dma((4,)),
+                dma((2, CHUNKS)),
                 dma((3,)),
                 dma((3,)),
                 dma((2, count)),
@@ -558,7 +635,7 @@
                 collective_id=0, has_side_effects=True, vmem_limit_bytes=58 * 1024 * 1024
             ),
             name="gather_and_multiply",
-        )(grad_out, out_weight, query_in, key_in, value_in, short_taps, modal_poles, modal_residues)
+        )(grad_out.reshape(SEGS, steps, -1), out_weight, query_in, key_in, value_in, short_taps, modal_poles, modal_residues)
     else:
         gathered_out = lax.all_gather(grad_out, "tp", axis=1, tiled=True)
         last = jnp.stack([x[tok_rows - rim :] for x in (query_in, key_in, value_in)])
@@ -584,32 +661,34 @@
         mixed = lax.dot_general(
             gathered_out, out_weight, (((1,), (1,)), ((), ())), preferred_element_type=F32
         )
-        ends, own = call(
-            backward_ends,
-            (mixed, qs, modal_poles),
-            (state_shape, own_shape),
-            [pltpu.VMEM((tok_rows, LANES), F32)],
-            work * 2 * modes,
-            "backward_ends",
+        ends, gq, gp, own = call(
+            backward_whole,
+            (mixed, qs, long_out, modal_poles, modal_residues),
+            (state_shape, seg_shape, seg_shape, own_shape),
+            [],
+            work * 4 * modes,
+            "backward_whole",
         )
         gathered = lax.all_gather(own, "ctx")
     gated, gq, gk, gv, heads, tails = call(
         backward_out,
-        (mine, mixed, qs, ks, vs, long_out, ends, gathered, short_taps,
+        (mine, gq, gp, qs, ks, vs, long_out, ends, gathered, short_taps,
          modal_poles, modal_residues),
         (plain, plain, plain, plain, rows_shape, rows_shape),
         [
             pltpu.VMEM((modes, SEGS, LANES), F32),
-            pltpu.VMEM((3, steps, SEGS, LANES), F32),
+            pltpu.VMEM((2, steps, SEGS, LANES), F32),
             pltpu.VMEM((tok_rows, LANES), F32),
         ],
-        work * (4 * modes + 6 * tap_count),
+        work * (2 * modes + 6 * tap_count),
         "backward_out",
         1,
+        60,
     )
     later = from_behind(heads, "ctx", -1)
+    beyond = jnp.pad(later, ((0, 0), (8, 0), (0, 0)))
     for j in range(1, tap_count):
-        tails = tails.at[:, 8 - j :, :].add(short_taps[:, j, None, :] * later[:, :j, :])
+        tails = tails + short_taps[:, j, None, :] * beyond[:, j : j + 8, :]
     tails = tails.astype(jnp.bfloat16)
     grads = [
         lax.dynamic_update_slice(g, tails[i], (tok_rows - 8, 0)) for i, g in enumerate((gq, gk, gv))

time: 248 us -> 209 us (0.84)
  Pallas kernels: 226 us -> 200 us
  local copies, waits for them, and re-layouts: 14.5 us -> 0.72 us
    pallas_call x1, Pallas kernels: 193 us -> 176 us  [shards(): pl.pallas_call(gather_and_multiply, out_shape=outputs, in_specs=[hbm] * 5...]
    unnamed x23 -> x5, local copies, waits for them, and re-layouts: 13 us -> 0.04 us
    pallas_call x1, Pallas kernels: 33.1 us -> 23.5 us  [call(): pl.pallas_call(body, grid=(outputs[0].shape[-1] // LANES,), in_specs=[pl....]
where the time goes in v2:
time: 209 us; the launch traced here: 208 us
  Pallas kernels  200 us (96%)
  waiting for transfers between devices  4.09 us (2%)
    pallas_call x1, Pallas kernels, shards(): pl.pallas_call(gather_and_multiply, out_shape=outputs, in_specs=[hbm] * 5...  176 us
    pallas_call x1, Pallas kernels, call(): pl.pallas_call(body, grid=(outputs[0].shape[-1] // LANES,), in_specs=[pl....  23.5 us
  transfers between devices with their start and end apart: 1, of which 1 were waited for; matrix products, arithmetic and copies ran while one was open for 0% of the time, Pallas kernels for 0%

profile of v2, /device:TPU:1, one launch (start us, length us, event | category | flops | bytes accessed | tf_op | source)
XLA Modules:
  0.0 208.4 jit_solution(9556368925007657633)
XLA Ops:
  0.6 176.5 %gather_and_multiply.1 = (f32[128,8,1024]{2,1,0:T(8,128)}, f32[128,8,1024]{2,1,0:T(8,128)}, f32[128,8,1024]{2,1,0:T(8,128)}, f32[128,8,1024]{2,1,0:T(8,128)}, f3...) custom-call(bf16[8,128,1024]{2,1,0:T(8,128)(2,1)} %bitcast.26, ...), custom_call_target="tpu_custom_call" | custom-call | flops 17179869184 | bytes 16777216 | tf_op jit(solution)/shard_map/gather_and_multiply/pallas_call | solution.py:600
  177.1 0.0 copy-start
  177.1 23.5 %backward_out.1 = (bf16[1024,1024]{1,0:T(8,128)(2,1)}, bf16[1024,1024]{1,0:T(8,128)(2,1)}, bf16[1024,1024]{1,0:T(8,128)(2,1)}, bf16[1024,1024]{1,0:T(8,128)(2,1)...) custom-call(s32[1]{0:T(128)} %bitcast.mine_ref, f32[128,8,1024]{2,1,0:T(8,128)} %get-tuple-element.18.grad_q_ref, ...), custom_call_target="tpu_custom_call" | custom-call | flops 77594624 | bytes 34754564 | tf_op jit(solution)/shard_map/backward_out/pallas_call | solution.py:561
  200.7 1.9 collective-permute-start
  202.6 0.0 copy-done
  202.6 0.1 fusion.16
  202.7 4.1 %collective-permute-done = f32[3,8,1024]{2,1,0:T(8,128)S(1)} collective-permute-done((f32[3,8,1024]{2,1,0:T(8,128)}, f32[3,8,1024]{2,1,0:T(8,128)S(1)}, u32[]{:S(2)}, u32[]{:S(2)}) %collective-permute-start) | collective-permute-done | bytes 98336 | tf_op jit(solution)/shard_map/ppermute | solution.py:20
  206.8 1.0 fusion.7
  207.8 0.6 fusion.13
  (3 shorter events, 0.0 us)
Async XLA Ops:
  177.1 25.5 %copy-start = (f32[3,7,1024]{2,1,0:T(8,128)S(1)}, f32[3,7,1024]{2,1,0:T(8,128)}, u32[]{:S(2)}) copy-start(f32[3,7,1024]{2,1,0:T(8,128)} %taps_ref.3) | copy-start | bytes 258052
  200.7 6.1 %collective-permute-start = (f32[3,8,1024]{2,1,0:T(8,128)}, f32[3,8,1024]{2,1,0:T(8,128)S(1)}, u32[]{:S(2)}, u32[]{:S(2)}) collective-permute-start(f32[3,8,1024]{2,1,0:T(8,128)} %get-tuple-element.29), channel_id=1, source_target_pairs={{8,0},{16,8},{24,16},{9,1},{17,9},{25,17},{10,2},{18,10},{26,18},{... | collective-permute-start | bytes 294920 | tf_op jit(solution)/shard_map/ppermute | solution.py:20
